TPU v7x, 32 devices: a whole 2x2x4 slice. The times are simulated.
32 devices in a mesh: grp: 4 (over y, x), dev: 8 (over z, core).
Axes of the slice: x: 2, y: 2, z: 4, core: 2. Of those that a mesh axis runs over, the one named last changes fastest.
Arguments:
- slab: bfloat16 [8, 8000, 8000], P('grp', 'dev'), may hold values from -2.5 to 2.5
- orbitals: bfloat16 [8000, 640], P('dev'), may hold values from -0.0625 to 0.0625
- hcore: float32 [8000, 8000], P('dev', 'grp'), may hold values from -6 to 6
- metric_inv: float32 [8, 8], replicated, may hold values from -1 to 2, as said below
Outputs:
- fock: float32 [8000, 8000], P('dev', 'grp')
Inputs may be any that keep to these rules, and one draw needn't show every extreme that they name: `metric_inv`: symmetric.
All inputs are finite; a program needn't handle non-finite values.
Results may differ from a plain program's by a relative error of at most 0.0065.
Values may be sent and summed in bfloat16 or wider, within the bound.
A program may use at most 192 MiB of HBM per device.

v0:
```python
import jax
import jax.numpy as jnp
from jax import lax
from jax.sharding import PartitionSpec as P


def shards(slab, orbitals, hcore, metric_inv):
    aux_count = slab.shape[0]
    row_count = slab.shape[1]
    full_width = slab.shape[2]
    occ_count = orbitals.shape[1]
    slab_flat = slab.reshape(aux_count * row_count, full_width)
    half_done = jnp.dot(
        slab_flat,
        lax.all_gather(orbitals, "dev", axis=0, tiled=True),
        preferred_element_type=jnp.float32,
    )
    half_done = half_done.astype(jnp.bfloat16).reshape(aux_count, row_count, occ_count)
    aux_density = jnp.sum(
        half_done.astype(jnp.float32) * orbitals.astype(jnp.float32)[None], axis=(1, 2)
    )
    group_index = lax.axis_index("grp")
    group_density = lax.psum(aux_density, "dev")
    density_all = lax.all_gather(group_density, "grp", axis=0, tiled=True)
    fit_coef = jnp.dot(metric_inv, density_all, precision=lax.Precision.HIGHEST)
    half_flat = jnp.transpose(half_done, (1, 0, 2)).reshape(row_count, aux_count * occ_count)
    exchange_part = lax.dot_general(
        half_flat,
        lax.all_gather(half_flat, "dev", axis=0, tiled=True),
        (((1,), (1,)), ((), ())),
        preferred_element_type=jnp.float32,
    )
    local_coef = lax.dynamic_slice_in_dim(fit_coef, group_index * aux_count, aux_count)
    coulomb_part = jnp.zeros((row_count, full_width), jnp.float32)
    for aux_index in range(aux_count):
        coulomb_part = coulomb_part + local_coef[aux_index] * slab[aux_index].astype(jnp.float32)
    reduced = lax.psum_scatter(
        2.0 * coulomb_part - exchange_part, "grp", scatter_dimension=1, tiled=True
    )
    fock = hcore + reduced
    return fock


def solution(mesh):
    return jax.shard_map(
        shards,
        mesh=mesh,
        in_specs=(P("grp", "dev", None), P("dev", None), P("dev", "grp"), P()),
        out_specs=P("dev", "grp"),
        check_vma=False,
    )
```

profile of v0, /device:TPU:0, one launch (start us, length us, event | category | flops | bytes accessed | tf_op | source)
XLA Modules:
  0.0 945.1 jit_solution(1383661688321132750)
XLA Ops:
  6.5 0.0 copy-start
  6.5 0.0 all-gather.3.cloned.1.call-start
  6.5 0.7 all-gather.3.cloned.1.call-update
  7.3 0.0 all-gather.5.cloned.1.call-start
  7.3 101.8 %all-gather.3.cloned.1.call-done = bf16[8000,640]{1,0:T(8,128)(2,1)} async-done(((bf16[1000,640]{1,0:T(8,128)(2,1)}), bf16[8000,640]{1,0:T(8,128)(2,1)}) %all-gather.3.cloned.1.call-update) | async-done | bytes 10240016 | tf_op jit(solution)/shard_map/all_gather | solution.py:15
  109.1 1.6 mul.37
  110.7 0.0 copy-start.2
  110.8 34.1 %multiply_reduce_fusion = (f32[2000]{0:T(1024)S(1)}, bf16[2000,640]{1,0:T(8,128)(2,1)}) fusion(f32[2000,640]{1,0:T(8,128)S(1)} %bitcast.26, bf16[2000,8000]{1,0:T(8,128)(2,1)} %bitcast.28, bf16[8000,640]{1,0:T(8,128)(2,1)} %all-gather.3.cloned.1.call-done), kind=kOutput, calls=%fused_computation.2 | convolution fusion | flops 20485117952 | bytes 49928000 | tf_op jit(solution)/shard_map/dot_general | solution.py:13
  144.8 3.0 copy.8
  147.8 2.7 copy.9
  150.5 0.0 all-gather.5.cloned.1.call-update
  150.5 0.0 all-reduce.4.cloned.1.call-start
  150.6 0.0 copy-done.2
  150.6 0.6 fusion.1
  151.2 0.1 reduce_sum.14
  151.3 0.1 reduce_sum.18
  152.1 14.2 %psum.7 = f32[2]{0:T(128)S(1)} all-reduce(f32[2]{0:T(128)S(1)} %reduce_sum.18), channel_id=1, replica_groups=mesh['grp'=4,'dev'=8] {'dev'}, use_global_device_ids=true, to_apply=%region_2.0 | all-reduce | flops 2 | bytes 16 | tf_op jit(solution)/shard_map/psum | solution.py:23
  166.3 0.2 dynamic-update-slice
  166.5 10.2 %all-reduce = f32[8]{0:T(128)S(1)} all-reduce(f32[8]{0:T(128)S(1)} %dynamic-update-slice), channel_id=1, replica_groups=mesh['grp'=4,'dev'=8] {'grp'}, use_global_device_ids=true, to_apply=%add | all-reduce | flops 8 | bytes 64
  176.7 0.0 copy-done
  176.7 0.1 convolution_bitcast_fusion
  176.8 0.1 dynamic_slice.3
  176.9 0.7 fusion.2
  177.6 153.0 %all-gather.5.cloned.1.call-done = bf16[8000,1280]{1,0:T(8,128)(2,1)} async-done(((bf16[1000,1280]{1,0:T(8,128)(2,1)}), bf16[8000,1280]{1,0:T(8,128)(2,1)}) %all-gather.5.cloned.1.call-update) | async-done | bytes 20480016 | tf_op jit(solution)/shard_map/all_gather | solution.py:29
  330.6 41.4 %bitcast_subtract_fusion = f32[1000,8000]{1,0:T(8,128)} fusion(bf16[1000,1280]{0,1:T(8,128)(2,1)S(1)} %bitcast.25, bf16[8000,1280]{1,0:T(8,128)(2,1)} %all-gather.5.cloned.1.call-done, bf16[2,1000,8000]{2,1,0:T(8,128)(2,1)} %param.4, f32[]{:T(128)} %bitcast.6, f32[]{:T(128)} %bitcast.5), kind=kOutput, calls=%fused_computation | convolution fusion | flops 20536000512 | bytes 87040008 | tf_op jit(solution)/shard_map/dot_general | solution.py:27
  372.0 0.0 all-reduce.4.cloned.1.call-update
  372.1 0.0 copy-start.1
  372.7 554.5 %all-reduce.4.cloned.1.call-done = f32[1000,8000]{1,0:T(8,128)} async-done(((f32[1000,8000]{1,0:T(8,128)}), f32[1000,8000]{1,0:T(8,128)}) %all-reduce.4.cloned.1.call-update) | async-done | bytes 32000016
  927.2 11.4 %dynamic-slice_add_fusion = f32[1000,2000]{1,0:T(8,128)} fusion(f32[1000,2000]{1,0:T(8,128)} %param.6, f32[1000,8000]{1,0:T(8,128)} %all-reduce.4.cloned.1.call-done, u32[]{:T(128)S(6)} %multiply.4), kind=kLoop, calls=%fused_computation.1 | loop fusion | flops 2000000 | bytes 24000004 | tf_op jit(solution)/shard_map/add | solution.py:40
  938.6 0.0 copy-done.1
  (1 shorter events, 0.0 us)
Async XLA Ops:
  6.5 170.2 %copy-start = (f32[8,8]{1,0:T(8,128)S(1)}, f32[8,8]{1,0:T(8,128)}, u32[]{:S(2)}) copy-start(f32[8,8]{1,0:T(8,128)} %param.7) | copy-start | bytes 772
  6.5 102.6 %all-gather.3.cloned.1.call-start = ((), (), s32[]{:S(2)}) async-start(), calls=%async_computation | async-start | bytes 11520000 | tf_op jit(solution)/shard_map/all_gather | solution.py:15
  7.3 323.4 %all-gather.5.cloned.1.call-start = ((), (), s32[]{:S(2)}) async-start(), calls=%async_computation.1 | async-start | bytes 23040000 | tf_op jit(solution)/shard_map/all_gather | solution.py:29
  110.7 39.9 %copy-start.2 = (u32[32]{0:T(128)S(1)}, u32[32]{0:T(128)}, u32[]{:S(2)}) copy-start(u32[32]{0:T(128)} %constant.18) | copy-start | bytes 388
  150.5 776.7 %all-reduce.4.cloned.1.call-start = ((), (), s32[]{:S(2)}) async-start(), calls=%async_computation.2 | async-start | bytes 64512000
  372.1 566.5 %copy-start.1 = (f32[8,8]{1,0:T(8,128)S(1)}, f32[8,8]{1,0:T(8,128)}, u32[]{:S(2)}) copy-start(f32[8,8]{1,0:T(8,128)} %param.7) | copy-start | bytes 772
Sparse Core Ops, SparseCore 0:
  9.0 100.0 all-gather.2
  150.7 179.9 all-gather.4
  372.2 554.9 all-reduce.3
where the time goes:
time: 945 us
  waiting for transfers between devices  810 us (86%)
  matrix products  75.6 us (8%)
  blocking collectives  24.4 us (3%)
  between operations  14.4 us (2%)
  other arithmetic  11.5 us (1%)
    unnamed x4, waiting for transfers between devices  555 us
    all_gather x1, waiting for transfers between devices, shards(): lax.all_gather(half_flat, 'dev', axis=0, tiled=True)  153 us
    all_gather x1, waiting for transfers between devices, shards(): lax.all_gather(orbitals, 'dev', axis=0, tiled=True)  102 us
    dot_general x1, matrix products, shards(): lax.dot_general(half_flat, lax.all_gather(half_flat, 'dev', axis=0, tiled...  41.4 us
    dot_general x1, matrix products, shards(): jnp.dot(slab_flat, lax.all_gather(orbitals, 'dev', axis=0, tiled=True), p...  34.1 us
  transfers between devices with their start and end apart: 3, of which 3 were waited for; matrix products, arithmetic and copies ran while one was open for 0% of the time, Pallas kernels for 0%

commit v1 on v0

v1 whole, which is shorter than its diff:
```python
import jax
import jax.numpy as jnp
from jax import lax
from jax.experimental.layout import Layout, with_layout_constraint
from jax.sharding import PartitionSpec as P

CHUNKS = 4


def by_rows(array):
    return with_layout_constraint(array, Layout(major_to_minor=tuple(range(array.ndim))))


def spans(row_count, chunks):
    step = -(-row_count // chunks)
    step = -(-step // 128) * 128
    return [(low, min(low + step, row_count)) for low in range(0, row_count, step)]


def gather_orbitals(orbitals, group_count):
    row_count = orbitals.shape[0]
    if row_count % group_count:
        return lax.all_gather(orbitals, "dev", axis=0, tiled=True)
    share = row_count // group_count
    mine = lax.dynamic_slice_in_dim(orbitals, lax.axis_index("grp") * share, share)
    return lax.all_gather(mine, ("dev", "grp"), axis=0, tiled=True)


def build(group_count, dev_count):
    per_group = dev_count // group_count

    def shards(slab, orbitals, hcore, metric_inv):
        aux_count, row_count, full_width = slab.shape
        group_index = lax.axis_index("grp")
        coefs = gather_orbitals(orbitals, group_count)
        pieces = spans(row_count, CHUNKS)

        halves, gathered = [], []
        density = jnp.zeros((aux_count,), jnp.float32)
        for low, high in pieces:
            by_aux = [
                by_rows(jnp.dot(slab[a, low:high], coefs, preferred_element_type=jnp.float32).astype(jnp.bfloat16))
                for a in range(aux_count)
            ]
            rows = orbitals[low:high].astype(jnp.float32)
            density = density + jnp.stack([jnp.sum(h.astype(jnp.float32) * rows) for h in by_aux])
            flat = by_rows(jnp.concatenate(by_aux, axis=1))
            halves.append(flat)
            gathered.append(by_rows(lax.all_gather(flat, "dev", axis=0, tiled=True)))
        half_flat = by_rows(jnp.concatenate(halves, axis=0))

        placed = lax.dynamic_update_slice_in_dim(
            jnp.zeros((aux_count * group_count,), jnp.float32), density, group_index * aux_count, 0
        )
        density_all = lax.psum(placed, ("grp", "dev"))
        fit_coef = jnp.dot(metric_inv, density_all, precision=lax.Precision.HIGHEST)
        local_coef = 2.0 * lax.dynamic_slice_in_dim(fit_coef, group_index * aux_count, aux_count)

        blocks = []
        for d in range(dev_count):
            cols = slice(d * row_count, (d + 1) * row_count)
            blocks.append(
                by_rows(sum(local_coef[a] * slab[a, :, cols].astype(jnp.float32) for a in range(aux_count)))
            )
        coulomb = by_rows(jnp.stack(blocks))

        sums = []
        for (low, high), whole in zip(pieces, gathered):
            width = high - low
            total = None
            for k in list(range(1, group_count)) + [0]:
                target = group_index ^ k
                others = lax.dynamic_slice_in_dim(whole, target * (per_group * width), per_group * width)
                exchange = lax.dot_general(
                    half_flat,
                    others,
                    (((1,), (1,)), ((), ())),
                    preferred_element_type=jnp.float32,
                )
                direct = lax.dynamic_slice(
                    coulomb, (target * per_group, 0, low), (per_group, row_count, width)
                )
                part = jnp.concatenate([direct[t] for t in range(per_group)], axis=1) - by_rows(exchange)
                if k:
                    pairs = [(g, g ^ k) for g in range(group_count)]
                    part = lax.ppermute(by_rows(part.astype(jnp.bfloat16)), "grp", pairs).astype(jnp.float32)
                total = part if total is None else total + part
            sums.append(by_rows(total))

        columns = []
        for t in range(per_group):
            for (low, high), total in zip(pieces, sums):
                width = high - low
                columns.append(total[:, t * width : (t + 1) * width])
        return hcore + by_rows(jnp.concatenate(columns, axis=1))

    return shards


def solution(mesh):
    return jax.shard_map(
        build(mesh.shape["grp"], mesh.shape["dev"]),
        mesh=mesh,
        in_specs=(P("grp", "dev", None), P("dev", None), P("dev", "grp"), P()),
        out_specs=P("dev", "grp"),
        check_vma=False,
    )
```

time: 945 us -> 563 us (0.60)
  waiting for transfers between devices: 810 us -> 186 us
  other arithmetic: 11.5 us -> 103 us
  local copies, waits for them, and re-layouts: 9.02 us -> 65.2 us
  matrix products: 75.6 us -> 130 us
  blocking collectives: 24.4 us -> 42.7 us
  starting transfers between devices: 0.08 us -> 16 us
    unnamed x4 -> x5, waiting for transfers between devices: 555 us -> 0.08 us
    all_gather x2 -> x5, waiting for transfers between devices: 255 us -> 91.4 us  [the longest x1 91.4 us: gather_orbitals(): return lax.all_gather(mine, ('dev', 'grp'), axis=0, tiled=True)]
    ppermute x0 -> x12, waiting for transfers between devices: none -> 94.6 us  [shards(): lax.ppermute(by_rows(part.astype(jnp.bfloat16)), 'grp', pairs)]
    unnamed x0 -> x7, other arithmetic: none -> 54.3 us
    dot_general x2 -> x24, matrix products: 75.5 us -> 130 us  [the longest x8 67.2 us: shards(): jnp.dot(slab[a, low:high], coefs, preferred_element_type=jnp.float32)]
    psum x1, blocking collectives: 14.2 us -> 42.7 us  [shards(): density_all = lax.psum(placed, ('grp', 'dev'))]
    squeeze x0 -> x2, local copies, waits for them, and re-layouts: none -> 24 us  [shards(): direct[t]]
    concatenate x0 -> x5, other arithmetic: none -> 20.6 us  [the longest x1 17 us: shards(): half_flat = by_rows(jnp.concatenate(halves, axis=0))]
  transfers between devices with their start and end apart: 3 -> 17, of which waited for: 3 -> 7; matrix products, arithmetic and copies ran while one was open for 0% -> 44% of each run, Pallas kernels for 0% -> 0%
where the time goes in v1:
time: 563 us; the launch traced here: 557 us
  waiting for transfers between devices  186 us (33%)
  matrix products  130 us (23%)
  other arithmetic  103 us (18%)
  local copies, waits for them, and re-layouts  65.2 us (12%)
  blocking collectives  42.7 us (8%)
  starting transfers between devices  16 us (3%)
  between operations  13.8 us (2%)
    ppermute x12, waiting for transfers between devices, shards(): lax.ppermute(by_rows(part.astype(jnp.bfloat16)), 'grp', pairs)  94.6 us
    all_gather x1, waiting for transfers between devices, gather_orbitals(): return lax.all_gather(mine, ('dev', 'grp'), axis=0, tiled=True)  91.4 us
    dot_general x8, matrix products, shards(): jnp.dot(slab[a, low:high], coefs, preferred_element_type=jnp.float32)  67.2 us
    dot_general x16, matrix products, shards(): lax.dot_general(half_flat, others, (((1,), (1,)), ((), ())), preferred_el...  62.4 us
    unnamed x7, other arithmetic  54.3 us
    psum x1, blocking collectives, shards(): density_all = lax.psum(placed, ('grp', 'dev'))  42.7 us
    squeeze x2, local copies, waits for them, and re-layouts, shards(): direct[t]  24 us
    concatenate x1, other arithmetic, shards(): half_flat = by_rows(jnp.concatenate(halves, axis=0))  17 us
  transfers between devices with their start and end apart: 17, of which 7 were waited for; matrix products, arithmetic and copies ran while one was open for 44% of the time, Pallas kernels for 0%

profile of v1, /device:TPU:0, one launch (start us, length us, event | category | flops | bytes accessed | tf_op | source)
XLA Modules:
  0.0 556.6 jit_solution(7558762890133327049)
XLA Ops:
  6.5 1.8 dynamic-slice_bitcast_fusion.32
  8.4 91.4 %all-gather.15.cloned.1.call-done = bf16[32,250,640]{2,1,0:T(8,128)(2,1)} async-done(((bf16[1,250,640]{2,1,0:T(8,128)(2,1)}), bf16[32,250,640]{2,1,0:T(8,128)(2,1)}) %all-gather.15.cloned.1.call-update) | async-done | bytes 10240016 | tf_op jit(solution)/shard_map/all_gather | solution.py:26
  99.8 10.9 %reshape.57 = bf16[8000,640]{1,0:T(8,128)(2,1)} reshape(bf16[32,250,640]{2,1,0:T(8,128)(2,1)} %all-gather.15.cloned.1.call-done) | data formatting | bytes 20480000
  110.7 8.2 %fusion.99 = bf16[232,640]{1,0:T(8,128)(2,1)S(1)} fusion(bf16[8000,640]{1,0:T(8,128)(2,1)} %reshape.57, bf16[2,1000,8000]{2,1,0:T(8,128)(2,1)} %param.4), kind=kOutput, calls=%fused_computation.96 | convolution fusion | flops 2375828480 | bytes 14278656 | tf_op jit(solution)/shard_map/dot_general | solution.py:42
  119.0 6.1 %fusion.111 = (f32[]{:T(128)}, f32[]{:T(128)}, bf16[232,640]{1,0:T(8,128)(2,1)S(1)}) fusion(bf16[1000,640]{1,0:T(8,128)(2,1)} %param.5, bf16[232,640]{1,0:T(8,128)(2,1)S(1)} %fusion.99, bf16[8000,640]{1,0:T(8,128)(2,1)S(1)} %copy-done.2, bf16[2,1000,8000]{2,1,0:T(8,128)(2,1)} %param.4), kind=kOutput, calls=%fused_computation.148 | convolution fusion | flops 2376867840 | bytes 14872584 | tf_op jit(solution)/shard_map/dot_general | solution.py:42
  126.9 8.6 %fusion.81 = bf16[256,640]{1,0:T(8,128)(2,1)S(1)} fusion(bf16[8000,640]{1,0:T(8,128)(2,1)} %reshape.57, bf16[2,1000,8000]{2,1,0:T(8,128)(2,1)} %param.4), kind=kOutput, calls=%fused_computation.90 | convolution fusion | flops 2621603840 | bytes 14696448 | tf_op jit(solution)/shard_map/dot_general | solution.py:42
  135.5 8.6 %fusion.84 = bf16[256,640]{1,0:T(8,128)(2,1)S(1)} fusion(bf16[8000,640]{1,0:T(8,128)(2,1)} %reshape.57, bf16[2,1000,8000]{2,1,0:T(8,128)(2,1)} %param.4), kind=kOutput, calls=%fused_computation.91 | convolution fusion | flops 2621603840 | bytes 14696448 | tf_op jit(solution)/shard_map/dot_general | solution.py:42
  145.1 8.7 %fusion.87 = bf16[256,640]{1,0:T(8,128)(2,1)S(1)} fusion(bf16[8000,640]{1,0:T(8,128)(2,1)} %reshape.57, bf16[2,1000,8000]{2,1,0:T(8,128)(2,1)} %param.4), kind=kOutput, calls=%fused_computation.92 | convolution fusion | flops 2621603840 | bytes 14696448 | tf_op jit(solution)/shard_map/dot_general | solution.py:42
  153.8 8.7 %fusion.90 = bf16[256,640]{1,0:T(8,128)(2,1)S(1)} fusion(bf16[8000,640]{1,0:T(8,128)(2,1)} %reshape.57, bf16[2,1000,8000]{2,1,0:T(8,128)(2,1)} %param.4), kind=kOutput, calls=%fused_computation.93 | convolution fusion | flops 2621603840 | bytes 14696448 | tf_op jit(solution)/shard_map/dot_general | solution.py:42
  163.8 8.7 %fusion.93 = bf16[256,640]{1,0:T(8,128)(2,1)S(1)} fusion(bf16[8000,640]{1,0:T(8,128)(2,1)} %reshape.57, bf16[2,1000,8000]{2,1,0:T(8,128)(2,1)} %param.4), kind=kOutput, calls=%fused_computation.94 | convolution fusion | flops 2621603840 | bytes 14696448 | tf_op jit(solution)/shard_map/dot_general | solution.py:42
  172.5 9.6 %fusion.105 = (f32[]{:T(128)}, f32[]{:T(128)}, f32[]{:T(128)}, f32[]{:T(128)}, f32[]{:T(128)}, /*index=5*/f32[]{:T(128)}, bf16[256,640]{1,0:T(8,128)(2,1)S(1)}) fusion(bf16[1000,640]{1,0:T(8,128)(2,1)} %param.5, bf16[256,640]{1,0:T(8,128)(2,1)S(1)} %fusion.93, bf16[256,640]{1,0:T(8,128)(2,1)S(1)} %fusion.87, bf16[256,640]{1,0:T(8,128)(2,1)S(1)} %fusion.81, ...), kind=kOutput, calls=%fused_computation.139 | convolution fusion | flops 2625044480 | bytes 17317912 | tf_op jit(solution)/shard_map/dot_general | solution.py:42
  182.1 5.1 fusion.132
  187.2 42.7 %psum.7 = f32[8]{0:T(128)S(1)} all-reduce(f32[8]{0:T(128)S(1)} %fusion.132), channel_id=1, replica_groups=mesh['grp'=4,'dev'=8] {'grp','dev'}, use_global_device_ids=true, to_apply=%region_8.0 | all-reduce | flops 8 | bytes 64 | tf_op jit(solution)/shard_map/psum | solution.py:55
  231.6 6.3 %add_dynamic-update-slice_fusion.7 = f32[8,1000,1000]{2,1,0:T(8,128)} fusion(bf16[2,1000,8000]{2,1,0:T(8,128)(2,1)} %param.4, f32[]{:T(128)} %bitcast.28, f32[]{:T(128)} %bitcast.27), kind=kLoop, calls=%fused_computation.25 | loop fusion | flops 4999999 | bytes 8096008
  237.9 8.0 %add_dynamic-update-slice_fusion.6 = f32[8,1000,1000]{2,1,0:T(8,128)} fusion(f32[8,1000,1000]{2,1,0:T(8,128)} %add_dynamic-update-slice_fusion.7, bf16[2,1000,8000]{2,1,0:T(8,128)(2,1)} %param.4, f32[]{:T(128)} %bitcast.28, f32[]{:T(128)} %bitcast.27), kind=kLoop, calls=%fused_computation.24 | loop fusion | flops 5000000 | bytes 8193024
  245.9 8.0 %add_dynamic-update-slice_fusion.5 = f32[8,1000,1000]{2,1,0:T(8,128)} fusion(f32[8,1000,1000]{2,1,0:T(8,128)} %add_dynamic-update-slice_fusion.6, bf16[2,1000,8000]{2,1,0:T(8,128)(2,1)} %param.4, f32[]{:T(128)} %bitcast.28, f32[]{:T(128)} %bitcast.27), kind=kLoop, calls=%fused_computation.23 | loop fusion | flops 5000000 | bytes 8193024
  253.9 8.0 %add_dynamic-update-slice_fusion.4 = f32[8,1000,1000]{2,1,0:T(8,128)} fusion(f32[8,1000,1000]{2,1,0:T(8,128)} %add_dynamic-update-slice_fusion.5, bf16[2,1000,8000]{2,1,0:T(8,128)(2,1)} %param.4, f32[]{:T(128)} %bitcast.28, f32[]{:T(128)} %bitcast.27), kind=kLoop, calls=%fused_computation.22 | loop fusion | flops 5000000 | bytes 8193024
  261.9 7.9 %add_dynamic-update-slice_fusion.3 = f32[8,1000,1000]{2,1,0:T(8,128)} fusion(f32[8,1000,1000]{2,1,0:T(8,128)} %add_dynamic-update-slice_fusion.4, bf16[2,1000,8000]{2,1,0:T(8,128)(2,1)} %param.4, f32[]{:T(128)} %bitcast.28, f32[]{:T(128)} %bitcast.27), kind=kLoop, calls=%fused_computation.21 | loop fusion | flops 5000000 | bytes 8193024
  269.9 8.1 %add_dynamic-update-slice_fusion.2 = f32[8,1000,1000]{2,1,0:T(8,128)} fusion(f32[8,1000,1000]{2,1,0:T(8,128)} %add_dynamic-update-slice_fusion.3, bf16[2,1000,8000]{2,1,0:T(8,128)(2,1)} %param.4, f32[]{:T(128)} %bitcast.28, f32[]{:T(128)} %bitcast.27), kind=kLoop, calls=%fused_computation.20 | loop fusion | flops 5000000 | bytes 8193024
  278.0 8.0 %add_dynamic-update-slice_fusion.1 = f32[8,1000,1000]{2,1,0:T(8,128)} fusion(f32[8,1000,1000]{2,1,0:T(8,128)} %add_dynamic-update-slice_fusion.2, bf16[2,1000,8000]{2,1,0:T(8,128)(2,1)} %param.4, f32[]{:T(128)} %bitcast.28, f32[]{:T(128)} %bitcast.27), kind=kLoop, calls=%fused_computation.19 | loop fusion | flops 5000000 | bytes 8193024
  286.0 7.9 %add_dynamic-update-slice_fusion = f32[8,1000,1000]{2,1,0:T(8,128)} fusion(f32[8,1000,1000]{2,1,0:T(8,128)} %add_dynamic-update-slice_fusion.1, bf16[2,1000,8000]{2,1,0:T(8,128)(2,1)} %param.4, f32[]{:T(128)} %bitcast.28, f32[]{:T(128)} %bitcast.27), kind=kLoop, calls=%fused_computation.18 | loop fusion | flops 5000000 | bytes 8193024 | tf_op jit(solution)/shard_map/stack | solution.py:65
  293.9 6.6 %dynamic-slice_bitcast_fusion.5 = (f32[1000,232]{1,0:T(8,128)}, f32[1000,232]{1,0:T(8,128)S(1)}, f32[1000,232]{1,0:T(8,128)}, f32[1000,232]{1,0:T(8,128)}, f32[1...) fusion(f32[8,1000,1000]{2,1,0:T(8,128)} %add_dynamic-update-slice_fusion, ...), kind=kLoop, calls=%fused_computation.104 | loop fusion | bytes 14848032 | tf_op jit(solution)/shard_map/squeeze | solution.py:83
  300.5 17.4 %dynamic-slice_bitcast_fusion.15 = (f32[1000,256]{1,0:T(8,128)}, f32[1000,256]{1,0:T(8,128)}, f32[1000,256]{1,0:T(8,128)}, f32[1000,256]{1,0:T(8,128)}, f32[1000...) fusion(f32[8,1000,1000]{2,1,0:T(8,128)} %add_dynamic-update-sli, ...), kind=kLoop, calls=%fused_computation.114 | loop fusion | bytes 49152032 | tf_op jit(solution)/shard_map/squeeze | solution.py:83
  317.9 17.0 %maximum_maximum_fusion = bf16[1000,1280]{1,0:T(8,128)(2,1)} fusion(bf16[232,640]{1,0:T(8,128)(2,1)S(1)} %fusion.99, bf16[232,640]{1,0:T(8,128)(2,1)S(1)} %copy-done.8, bf16[256,640]{1,0:T(8,128)(2,1)S(1)} %fusion.81, bf16[256,640]{1,0:T(8,128)(2,1)S(1)} %fusion.84, bf16[256,640]{1,0:T(8,128)(2,1)S(1)} %fusion.87, bf16[256,640]{1,0:T(8,128)(2,1)S(1)} %fusion.90, ...), kind=kLoop, calls=%fused_computation.32 | loop fusion | flops 20480000 | bytes 5120000 | tf_op jit(solution)/shard_map/concatenate | solution.py:50
  334.9 4.2 fusion.37
  339.2 1.5 copy.12
  340.6 2.3 collective-permute-start.10
  342.9 5.3 fusion.36
  348.3 2.7 copy.11
  351.9 4.6 fusion.38
  356.5 2.3 copy.15
  359.4 4.9 fusion.76
  364.3 4.8 fusion.32
  369.1 2.0 collective-permute-start.6
  371.1 4.0 fusion.33
  376.0 4.8 fusion.28
  381.4 2.5 fusion.29
  383.9 4.0 fusion.34
  388.0 2.5 fusion.30
  390.5 4.7 fusion.24
  395.9 2.6 fusion.25
  399.2 2.6 fusion.26
  401.8 2.2 copy.13
  404.0 2.0 collective-permute-start.3
  406.0 1.7 copy.14
  408.6 2.4 copy.16
  411.1 3.6 fusion.39
  414.7 3.0 collective-permute-done.6
  417.7 1.5 collective-permute-start.5
  419.6 19.5 %collective-permute-done.8 = bf16[1000,512]{1,0:T(8,128)(2,1)} collective-permute-done((bf16[1000,512]{1,0:T(8,128)(2,1)}, bf16[1000,512]{1,0:T(8,128)(2,1)}, u32[]{:S(2)}, u32[]{:S(2)}) %collective-permute-start.8) | collective-permute-done | bytes 1024032 | tf_op jit(solution)/shard_map/ppermute | solution.py:86
  439.1 2.0 collective-permute-start.1
  441.1 4.1 fusion.35
  445.2 16.4 %collective-permute-done.3 = bf16[1000,512]{1,0:T(8,128)(2,1)} collective-permute-done((bf16[1000,512]{1,0:T(8,128)(2,1)}, bf16[1000,512]{1,0:T(8,128)(2,1)}, u32[]{:S(2)}, u32[]{:S(2)}) %collective-permute-start.3) | collective-permute-done | bytes 1024032 | tf_op jit(solution)/shard_map/ppermute | solution.py:86
  461.6 1.5 collective-permute-start.2
  463.1 1.1 fusion.134
  464.3 18.7 %collective-permute-done.5 = bf16[1000,512]{1,0:T(8,128)(2,1)S(1)} collective-permute-done((bf16[1000,512]{1,0:T(8,128)(2,1)S(1)}, bf16[1000,512]{1,0:T(8,128)(2,1)S(1)}, u32[]{:S(2)}, u32[]{:S(2)}) %collective-permute-start.5) | collective-permute-done | bytes 1024032 | tf_op jit(solution)/shard_map/ppermute | solution.py:86
  483.0 3.7 fusion.31
  486.7 1.5 fusion.135
  488.2 17.3 %collective-permute-done = bf16[1000,512]{1,0:T(8,128)(2,1)S(1)} collective-permute-done((bf16[1000,512]{1,0:T(8,128)(2,1)S(1)}, bf16[1000,512]{1,0:T(8,128)(2,1)S(1)}, u32[]{:S(2)}, u32[]{:S(2)}) %collective-permute-start) | collective-permute-done | bytes 1024032 | tf_op jit(solution)/shard_map/ppermute | solution.py:86
  505.4 19.7 %collective-permute-done.2 = bf16[1000,512]{1,0:T(8,128)(2,1)S(1)} collective-permute-done((bf16[1000,512]{1,0:T(8,128)(2,1)S(1)}, bf16[1000,512]{1,0:T(8,128)(2,1)S(1)}, u32[]{:S(2)}, u32[]{:S(2)}) %collective-permute-start.2) | collective-permute-done | bytes 1024032 | tf_op jit(solution)/shard_map/ppermute | solution.py:86
  525.2 3.1 fusion.27
  528.2 1.4 fusion.136
  529.7 8.6 %concatenate.87 = f32[1000,2000]{1,0:T(8,128)} concatenate(f32[1000,256]{1,0:T(8,128)} %get-tuple-element.52, f32[1000,256]{1,0:T(8,128)} %get-tuple-element.50, f32[1000,256]{1,0:T(8,128)} %get-tuple-element.48, f32[1000,232]{1,0:T(8,128)S(1)} %get-tuple-element.46, f32[1000,256]{1,0:T(8,128)} %get-tuple-element.51, f32[1000,256]{1,0:T(8,128)} %get-tuple-element.49, ...), dimensions={1} | concatenate | bytes 16000000 | tf_op jit(solution)/shard_map/concatenate | solution.py:95
  538.3 11.6 %add.203 = f32[1000,2000]{1,0:T(8,128)} add(f32[1000,2000]{1,0:T(8,128)} %param.6, f32[1000,2000]{1,0:T(8,128)} %concatenate.87) | non-fusion elementwise | flops 2000000 | bytes 24000000 | tf_op jit(solution)/shard_map/add | solution.py:95
  (117 shorter events, 11.6 us)
Async XLA Ops:
  6.5 223.3 %copy-start = (f32[8,8]{1,0:T(8,128)S(1)}, f32[8,8]{1,0:T(8,128)}, u32[]{:S(2)}) copy-start(f32[8,8]{1,0:T(8,128)} %param.7) | copy-start | bytes 772
  6.5 93.3 %all-gather.15.cloned.1.call-start = ((), (), s32[]{:S(2)}) async-start(), calls=%async_computation.4 | async-start | bytes 10813440 | tf_op jit(solution)/shard_map/all_gather | solution.py:26
  8.4 326.6 %all-gather.13.cloned.1.call-start = ((), (), s32[]{:S(2)}) async-start(), calls=%async_computation.3 | async-start | bytes 5345280 | tf_op jit(solution)/shard_map/all_gather | solution.py:49
  110.7 8.2 %copy-start.2 = (bf16[8000,640]{1,0:T(8,128)(2,1)S(1)}, bf16[8000,640]{1,0:T(8,128)(2,1)}, u32[]{:S(2)}) copy-start(bf16[8000,640]{1,0:T(8,128)(2,1)} %reshape.57) | copy-start | bytes 30720004
  125.1 0.7 copy-start.7
  126.7 237.6 %all-gather.11.cloned.1.call-start = ((), (), s32[]{:S(2)}) async-start(), calls=%async_computation.2 | async-start | bytes 5898240 | tf_op jit(solution)/shard_map/all_gather | solution.py:49
  145.1 230.9 %all-gather.9.cloned.1.call-start = ((), (), s32[]{:S(2)}) async-start(), calls=%async_computation.1 | async-start | bytes 5898240 | tf_op jit(solution)/shard_map/all_gather | solution.py:49
  163.5 227.0 %all-gather.7.cloned.1.call-start = ((), (), s32[]{:S(2)}) async-start(), calls=%async_computation | async-start | bytes 5898240 | tf_op jit(solution)/shard_map/all_gather | solution.py:49
  300.5 17.4 %copy-start.8 = (bf16[232,640]{1,0:T(8,128)(2,1)S(1)}, bf16[232,640]{1,0:T(8,128)(2,1)}, u32[]{:S(2)}) copy-start(bf16[232,640]{1,0:T(8,128)(2,1)} %copy-done.7) | copy-start | bytes 890884
  340.6 57.9 %collective-permute-start.10 = (bf16[1000,464]{0,1:T(8,128)(2,1)}, bf16[1000,464]{0,1:T(8,128)(2,1)}, u32[]{:S(2)}, u32[]{:S(2)}) collective-permute-start(bf16[1000,464]{0,1:T(8,128)(2,1)} %copy.12), channel_id=1, source_target_pairs={{0,16},{8,24},{16,0},{24,8},{1,17},{9,25},{17,1},{25,9},{2,18},{10... | collective-permute-start | bytes 2784008 | tf_op jit(solution)/shard_map/ppermute | solution.py:86
  342.9 9.0 %copy-start.33 = (f32[1000,232]{1,0:T(8,128)S(1)}, f32[1000,232]{1,0:T(8,128)}, u32[]{:S(2)}) copy-start(f32[1000,232]{1,0:T(8,128)} %get-tuple-element.15) | copy-start | bytes 2784004
  342.9 9.0 %copy-start.34 = (f32[1000,232]{1,0:T(8,128)S(1)}, f32[1000,232]{1,0:T(8,128)}, u32[]{:S(2)}) copy-start(f32[1000,232]{1,0:T(8,128)} %get-tuple-element.17) | copy-start | bytes 2784004
  350.9 53.1 %collective-permute-start.9 = (bf16[1000,464]{0,1:T(8,128)(2,1)}, bf16[1000,464]{0,1:T(8,128)(2,1)}, u32[]{:S(2)}, u32[]{:S(2)}) collective-permute-start(bf16[1000,464]{0,1:T(8,128)(2,1)} %copy.11), channel_id=1, source_target_pairs={{0,8},{8,0},{16,24},{24,16},{1,9},{9,1},{17,25},{25,17},{2,10},{10... | collective-permute-start | bytes 2784008 | tf_op jit(solution)/shard_map/ppermute | solution.py:86
  358.8 5.5 copy-start.31
  358.8 5.5 copy-start.32
  358.8 49.0 %collective-permute-start.11 = (bf16[1000,464]{0,1:T(8,128)(2,1)}, bf16[1000,464]{0,1:T(8,128)(2,1)}, u32[]{:S(2)}, u32[]{:S(2)}) collective-permute-start(bf16[1000,464]{0,1:T(8,128)(2,1)} %copy.15), channel_id=1, source_target_pairs={{0,24},{8,16},{16,8},{24,0},{1,25},{9,17},{17,9},{25,1},{2,26},{10... | collective-permute-start | bytes 2784008 | tf_op jit(solution)/shard_map/ppermute | solution.py:86
  364.3 6.8 %copy-start.3 = (bf16[1000,1280]{1,0:T(8,128)(2,1)S(1)}, bf16[1000,1280]{1,0:T(8,128)(2,1)}, u32[]{:S(2)}) copy-start(bf16[1000,1280]{1,0:T(8,128)(2,1)} %maximum_maximum_fusion) | copy-start | bytes 7680004
  364.3 6.8 %copy-start.29 = (f32[1000,256]{1,0:T(8,128)S(1)}, f32[1000,256]{1,0:T(8,128)}, u32[]{:S(2)}) copy-start(f32[1000,256]{1,0:T(8,128)} %get-tuple-element.24) | copy-start | bytes 3072004
  364.3 6.8 %copy-start.30 = (f32[1000,256]{1,0:T(8,128)S(1)}, f32[1000,256]{1,0:T(8,128)}, u32[]{:S(2)}) copy-start(f32[1000,256]{1,0:T(8,128)} %get-tuple-element.35) | copy-start | bytes 3072004
  369.1 48.6 %collective-permute-start.6 = (bf16[1000,512]{1,0:T(8,128)(2,1)}, bf16[1000,512]{1,0:T(8,128)(2,1)}, u32[]{:S(2)}, u32[]{:S(2)}) collective-permute-start(bf16[1000,512]{1,0:T(8,128)(2,1)} %fusion.32), channel_id=1, source_target_pairs={{0,8},{8,0},{16,24},{24,16},{1,9},{9,1},{17,25},{25,17},{2,10},{10... | collective-permute-start | bytes 3072008 | tf_op jit(solution)/shard_map/ppermute | solution.py:86
  371.1 4.8 copy-start.27
  371.1 4.8 copy-start.28
  375.1 44.4 %collective-permute-start.7 = (bf16[1000,512]{1,0:T(8,128)(2,1)}, bf16[1000,512]{1,0:T(8,128)(2,1)}, u32[]{:S(2)}, u32[]{:S(2)}) collective-permute-start(bf16[1000,512]{1,0:T(8,128)(2,1)} %fusion.33), channel_id=1, source_target_pairs={{0,16},{8,24},{16,0},{24,8},{1,17},{9,25},{17,1},{25,9},{2,18},{10... | collective-permute-start | bytes 3072008 | tf_op jit(solution)/shard_map/ppermute | solution.py:86
  375.9 4.8 copy-start.4
  375.9 4.8 copy-start.25
  376.0 4.8 copy-start.26
  376.0 5.4 copy-start.35
  381.4 2.5 copy-start.23
  381.4 2.5 copy-start.24
  383.9 4.0 copy-start.21
  383.9 4.0 copy-start.22
  387.9 2.6 copy-start.19
  388.0 2.6 copy-start.20
  390.5 4.8 copy-start.5
  390.5 4.8 copy-start.17
  390.5 4.8 copy-start.18
  390.5 5.4 copy-start.36
  395.9 3.2 copy-start.15
  395.9 3.2 copy-start.16
  398.5 40.6 %collective-permute-start.8 = (bf16[1000,512]{1,0:T(8,128)(2,1)}, bf16[1000,512]{1,0:T(8,128)(2,1)}, u32[]{:S(2)}, u32[]{:S(2)}) collective-permute-start(bf16[1000,512]{1,0:T(8,128)(2,1)} %fusion.34), channel_id=1, source_target_pairs={{0,24},{8,16},{16,8},{24,0},{1,25},{9,17},{17,9},{25,1},{2,26},{10... | collective-permute-start | bytes 3072008 | tf_op jit(solution)/shard_map/ppermute | solution.py:86
  404.0 57.6 %collective-permute-start.3 = (bf16[1000,512]{1,0:T(8,128)(2,1)}, bf16[1000,512]{1,0:T(8,128)(2,1)}, u32[]{:S(2)}, u32[]{:S(2)}) collective-permute-start(bf16[1000,512]{1,0:T(8,128)(2,1)} %fusion.28), channel_id=1, source_target_pairs={{0,8},{8,0},{16,24},{24,16},{1,9},{9,1},{17,25},{25,17},{2,10},{10... | collective-permute-start | bytes 3072008 | tf_op jit(solution)/shard_map/ppermute | solution.py:86
  407.7 56.5 %collective-permute-start.4 = (bf16[1000,512]{1,0:T(8,128)(2,1)}, bf16[1000,512]{1,0:T(8,128)(2,1)}, u32[]{:S(2)}, u32[]{:S(2)}) collective-permute-start(bf16[1000,512]{1,0:T(8,128)(2,1)} %fusion.29), channel_id=1, source_target_pairs={{0,16},{8,24},{16,0},{24,8},{1,17},{9,25},{17,1},{25,9},{2,18},{10... | collective-permute-start | bytes 3072008 | tf_op jit(solution)/shard_map/ppermute | solution.py:86
  411.0 6.6 %copy-start.39 = (bf16[1000,512]{1,0:T(8,128)(2,1)S(1)}, bf16[1000,512]{1,0:T(8,128)(2,1)}, u32[]{:S(2)}) copy-start(bf16[1000,512]{1,0:T(8,128)(2,1)} %fusion.30) | copy-start | bytes 3072004
  411.1 8.5 %copy-start.37 = (bf16[1000,512]{1,0:T(8,128)(2,1)S(1)}, bf16[1000,512]{1,0:T(8,128)(2,1)}, u32[]{:S(2)}) copy-start(bf16[1000,512]{1,0:T(8,128)(2,1)} %fusion.24) | copy-start | bytes 3072004
  411.1 28.1 %copy-start.38 = (bf16[1000,512]{1,0:T(8,128)(2,1)S(1)}, bf16[1000,512]{1,0:T(8,128)(2,1)}, u32[]{:S(2)}) copy-start(bf16[1000,512]{1,0:T(8,128)(2,1)} %fusion.25) | copy-start | bytes 3072004
  411.1 30.0 %copy-start.14 = (f32[1000,256]{1,0:T(8,128)S(1)}, f32[1000,256]{1,0:T(8,128)}, u32[]{:S(2)}) copy-start(f32[1000,256]{1,0:T(8,128)} %get-tuple-element.33) | copy-start | bytes 3072004
  414.6 26.5 %copy-start.6 = (bf16[1000,1280]{1,0:T(8,128)(2,1)S(1)}, bf16[1000,1280]{1,0:T(8,128)(2,1)}, u32[]{:S(2)}) copy-start(bf16[1000,1280]{1,0:T(8,128)(2,1)} %maximum_maximum_fusion) | copy-start | bytes 7680004
  414.7 26.5 %copy-start.13 = (f32[1000,256]{1,0:T(8,128)S(1)}, f32[1000,256]{1,0:T(8,128)}, u32[]{:S(2)}) copy-start(f32[1000,256]{1,0:T(8,128)} %get-tuple-element.22) | copy-start | bytes 3072004
  417.7 65.3 %collective-permute-start.5 = (bf16[1000,512]{1,0:T(8,128)(2,1)S(1)}, bf16[1000,512]{1,0:T(8,128)(2,1)S(1)}, u32[]{:S(2)}, u32[]{:S(2)}) collective-permute-start(bf16[1000,512]{1,0:T(8,128)(2,1)S(1)} %copy-done.39), channel_id=1, source_target_pairs={{0,24},{8,16},{16,8},{24,0},{1,25},{9,17},{17,9},{25,1},{2,26},{10... | collective-permute-start | bytes 3072008 | tf_op jit(solution)/shard_map/ppermute | solution.py:86
  419.5 85.9 %collective-permute-start = (bf16[1000,512]{1,0:T(8,128)(2,1)S(1)}, bf16[1000,512]{1,0:T(8,128)(2,1)S(1)}, u32[]{:S(2)}, u32[]{:S(2)}) collective-permute-start(bf16[1000,512]{1,0:T(8,128)(2,1)S(1)} %copy-done.37), channel_id=1, source_target_pairs={{0,8},{8,0},{16,24},{24,16},{1,9},{9,1},{17,25},{25,17},{2,10},{10... | collective-permute-start | bytes 3072008 | tf_op jit(solution)/shard_map/ppermute | solution.py:86
  439.1 66.3 %collective-permute-start.1 = (bf16[1000,512]{1,0:T(8,128)(2,1)S(1)}, bf16[1000,512]{1,0:T(8,128)(2,1)S(1)}, u32[]{:S(2)}, u32[]{:S(2)}) collective-permute-start(bf16[1000,512]{1,0:T(8,128)(2,1)S(1)} %copy-done.38), channel_id=1, source_target_pairs={{0,16},{8,24},{16,0},{24,8},{1,17},{9,25},{17,1},{25,9},{2,18},{10... | collective-permute-start | bytes 3072008 | tf_op jit(solution)/shard_map/ppermute | solution.py:86
  441.1 20.5 %copy-start.40 = (bf16[1000,512]{1,0:T(8,128)(2,1)S(1)}, bf16[1000,512]{1,0:T(8,128)(2,1)}, u32[]{:S(2)}) copy-start(bf16[1000,512]{1,0:T(8,128)(2,1)} %fusion.26) | copy-start | bytes 3072004
  445.2 37.8 %copy-start.11 = (f32[1000,256]{1,0:T(8,128)S(1)}, f32[1000,256]{1,0:T(8,128)}, u32[]{:S(2)}) copy-start(f32[1000,256]{1,0:T(8,128)} %get-tuple-element.25) | copy-start | bytes 3072004
  445.2 37.8 %copy-start.12 = (f32[1000,256]{1,0:T(8,128)S(1)}, f32[1000,256]{1,0:T(8,128)}, u32[]{:S(2)}) copy-start(f32[1000,256]{1,0:T(8,128)} %get-tuple-element.37) | copy-start | bytes 3072004
  461.6 63.6 %collective-permute-start.2 = (bf16[1000,512]{1,0:T(8,128)(2,1)S(1)}, bf16[1000,512]{1,0:T(8,128)(2,1)S(1)}, u32[]{:S(2)}, u32[]{:S(2)}) collective-permute-start(bf16[1000,512]{1,0:T(8,128)(2,1)S(1)} %copy-done.40), channel_id=1, source_target_pairs={{0,24},{8,16},{16,8},{24,0},{1,25},{9,17},{17,9},{25,1},{2,26},{10... | collective-permute-start | bytes 3072008 | tf_op jit(solution)/shard_map/ppermute | solution.py:86
  486.7 38.5 %copy-start.9 = (f32[1000,256]{1,0:T(8,128)S(1)}, f32[1000,256]{1,0:T(8,128)}, u32[]{:S(2)}) copy-start(f32[1000,256]{1,0:T(8,128)} %get-tuple-element.29) | copy-start | bytes 3072004
  486.7 38.5 %copy-start.10 = (f32[1000,256]{1,0:T(8,128)S(1)}, f32[1000,256]{1,0:T(8,128)}, u32[]{:S(2)}) copy-start(f32[1000,256]{1,0:T(8,128)} %get-tuple-element.41) | copy-start | bytes 3072004
  538.3 11.6 %copy-start.1 = (f32[8,8]{1,0:T(8,128)S(1)}, f32[8,8]{1,0:T(8,128)}, u32[]{:S(2)}) copy-start(f32[8,8]{1,0:T(8,128)} %param.7) | copy-start | bytes 772
Sparse Core Ops, SparseCore 0:
  10.2 89.5 all-gather.14
  126.8 50.4 all-gather.12
  179.0 55.8 all-gather.10
  236.3 54.7 all-gather.8
  292.6 54.8 all-gather.6

commit v2 on v1

v2 whole, which is shorter than its diff:
```python
import jax
import jax.numpy as jnp
from jax import lax
from jax.experimental.layout import Layout, with_layout_constraint
from jax.sharding import PartitionSpec as P

CHUNKS = 4


def by_rows(array):
    return with_layout_constraint(array, Layout(major_to_minor=tuple(range(array.ndim))))


def spans(row_count, chunks):
    step = -(-row_count // chunks)
    step = -(-step // 128) * 128
    return [(low, min(low + step, row_count)) for low in range(0, row_count, step)]


def build(group_count, dev_count):
    per_group = dev_count // group_count

    def shards(slab, orbitals, hcore, metric_inv):
        aux_count, row_count, full_width = slab.shape
        group_index = lax.axis_index("grp")
        coefs = lax.all_gather(orbitals, "dev", axis=0, tiled=True)
        pieces = spans(row_count, CHUNKS)

        halves, gathered = [], []
        density = jnp.zeros((aux_count,), jnp.float32)
        for low, high in pieces:
            by_aux = [
                by_rows(jnp.dot(slab[a, low:high], coefs, preferred_element_type=jnp.float32).astype(jnp.bfloat16))
                for a in range(aux_count)
            ]
            rows = orbitals[low:high].astype(jnp.float32)
            density = density + jnp.stack([jnp.sum(h.astype(jnp.float32) * rows) for h in by_aux])
            flat = by_rows(jnp.concatenate(by_aux, axis=1))
            flat, coefs = lax.optimization_barrier((flat, coefs))
            halves.append(flat)
            gathered.append(by_rows(lax.all_gather(flat, "dev", axis=0, tiled=True)))
        half_flat = by_rows(jnp.concatenate(halves, axis=0))

        placed = lax.dynamic_update_slice_in_dim(
            jnp.zeros((aux_count * group_count,), jnp.float32), density, group_index * aux_count, 0
        )
        density_all = lax.psum(placed, ("grp", "dev"))
        fit_coef = jnp.dot(metric_inv, density_all, precision=lax.Precision.HIGHEST)
        local_coef = 2.0 * lax.dynamic_slice_in_dim(fit_coef, group_index * aux_count, aux_count)

        fock = hcore
        received = []
        for index, ((low, high), whole) in enumerate(zip(pieces, gathered)):
            width = high - low
            if index >= 2:
                *landed, local_coef = lax.optimization_barrier((*received[index - 2], local_coef))
                received[index - 2] = landed
            blocks = []
            for d in range(dev_count):
                cols = slice(d * row_count + low, d * row_count + high)
                blocks.append(
                    by_rows(sum(local_coef[a] * slab[a, :, cols].astype(jnp.float32) for a in range(aux_count)))
                )
            coulomb = by_rows(jnp.stack(blocks))
            parts = []
            for k in list(range(1, group_count)) + [0]:
                target = group_index ^ k
                others = lax.dynamic_slice_in_dim(whole, target * (per_group * width), per_group * width)
                exchange = lax.dot_general(
                    half_flat, others, (((1,), (1,)), ((), ())), preferred_element_type=jnp.float32
                )
                direct = lax.dynamic_slice_in_dim(coulomb, target * per_group, per_group)
                part = jnp.concatenate([direct[t] for t in range(per_group)], axis=1) - by_rows(exchange)
                parts.append(by_rows(part.astype(jnp.bfloat16)) if k else by_rows(part))
            *parts, local_coef = lax.optimization_barrier((*parts, local_coef))
            for k in range(1, group_count):
                pairs = [(g, g ^ k) for g in range(group_count)]
                parts[k - 1] = lax.ppermute(parts[k - 1], "grp", pairs)
            received.append(parts)
        for (low, high), parts in zip(pieces, received):
            width = high - low
            total = parts[-1]
            for part in parts[:-1]:
                total = total + part.astype(jnp.float32)
            for t in range(per_group):
                first = t * row_count + low
                block = hcore[:, first : first + width] + total[:, t * width : (t + 1) * width]
                fock = lax.dynamic_update_slice(fock, block, (0, first))
        return fock

    return shards


def solution(mesh):
    return jax.shard_map(
        build(mesh.shape["grp"], mesh.shape["dev"]),
        mesh=mesh,
        in_specs=(P("grp", "dev", None), P("dev", None), P("dev", "grp"), P()),
        out_specs=P("dev", "grp"),
        check_vma=False,
    )
```

time: 563 us -> 552 us (0.980)
  waiting for transfers between devices: 186 us -> 123 us
  other arithmetic: 103 us -> 135 us
  matrix products: 130 us -> 141 us
  local copies, waits for them, and re-layouts: 65.2 us -> 71.6 us
    ppermute x12, waiting for transfers between devices: 94.6 us -> 20.6 us  [shards(): parts[k - 1] = lax.ppermute(parts[k - 1], 'grp', pairs)]
    unnamed x7 -> x28, other arithmetic: 54.3 us -> 91.7 us
    dynamic_update_slice x0 -> x5, local copies, waits for them, and re-layouts: none -> 31.6 us  [shards(): fock = lax.dynamic_update_slice(fock, block, (0, first))]
    concatenate x1 -> x0, other arithmetic: 17 us -> none  [shards(): half_flat = by_rows(jnp.concatenate(halves, axis=0))]
    dot_general x16, matrix products: 62.4 us -> 73.9 us  [shards(): lax.dot_general(half_flat, others, (((1,), (1,)), ((), ())), preferred_el...]
    all_gather x1, waiting for transfers between devices: 91.4 us -> 102 us  [shards(): coefs = lax.all_gather(orbitals, 'dev', axis=0, tiled=True)]
    squeeze x2 -> x4, local copies, waits for them, and re-layouts: 24 us -> 14.8 us  [shards(): direct[t]]
    concatenate x1, local copies, waits for them, and re-layouts: 8.59 us -> 0.86 us  [shards(): half_flat = by_rows(jnp.concatenate(halves, axis=0))]
  transfers between devices with their start and end apart: 17 -> 17, of which waited for: 7 -> 5; matrix products, arithmetic and copies ran while one was open for 44% -> 57% of each run, Pallas kernels for 0% -> 0%
where the time goes in v2:
time: 552 us; the launch traced here: 542 us
  matrix products  141 us (26%)
  other arithmetic  135 us (24%)
  waiting for transfers between devices  123 us (22%)
  local copies, waits for them, and re-layouts  71.6 us (13%)
  blocking collectives  42 us (8%)
  starting transfers between devices  15 us (3%)
  between operations  13.8 us (2%)
    all_gather x1, waiting for transfers between devices, shards(): coefs = lax.all_gather(orbitals, 'dev', axis=0, tiled=True)  102 us
    unnamed x28, other arithmetic  91.7 us
    dot_general x16, matrix products, shards(): lax.dot_general(half_flat, others, (((1,), (1,)), ((), ())), preferred_el...  73.9 us
    dot_general x8, matrix products, shards(): jnp.dot(slab[a, low:high], coefs, preferred_element_type=jnp.float32)  66.9 us
    psum x1, blocking collectives, shards(): density_all = lax.psum(placed, ('grp', 'dev'))  42 us
    dynamic_update_slice x5, local copies, waits for them, and re-layouts, shards(): fock = lax.dynamic_update_slice(fock, block, (0, first))  31.6 us
    ppermute x12, waiting for transfers between devices, shards(): parts[k - 1] = lax.ppermute(parts[k - 1], 'grp', pairs)  20.6 us
    squeeze x4, local copies, waits for them, and re-layouts, shards(): direct[t]  14.8 us
  transfers between devices with their start and end apart: 17, of which 5 were waited for; matrix products, arithmetic and copies ran while one was open for 57% of the time, Pallas kernels for 0%

profile of v2, /device:TPU:0, one launch (start us, length us, event | category | flops | bytes accessed | tf_op | source)
XLA Modules:
  0.0 541.6 jit_solution(5754998785579124811)
XLA Ops:
  7.3 101.8 %all-gather.6.cloned.1.call-done = bf16[8000,640]{1,0:T(8,128)(2,1)} async-done(((bf16[1000,640]{1,0:T(8,128)(2,1)}), bf16[8000,640]{1,0:T(8,128)(2,1)}) %all-gather.6.cloned.1.call-update) | async-done | bytes 10240016 | tf_op jit(solution)/shard_map/all_gather | solution.py:26
  109.1 8.7 %fusion.48 = bf16[256,640]{1,0:T(8,128)(2,1)S(1)} fusion(bf16[8000,640]{1,0:T(8,128)(2,1)} %all-gather.6.cloned.1.call-done, bf16[2,1000,8000]{2,1,0:T(8,128)(2,1)} %param.4), kind=kOutput, calls=%fused_computation.68 | convolution fusion | flops 2621603840 | bytes 14696448 | tf_op jit(solution)/shard_map/dot_general | solution.py:33
  117.8 5.6 %fusion.51 = bf16[256,640]{1,0:T(8,128)(2,1)S(1)} fusion(bf16[8000,640]{1,0:T(8,128)(2,1)S(1)} %copy-done.27, bf16[2,1000,8000]{2,1,0:T(8,128)(2,1)} %param.4), kind=kOutput, calls=%fused_computation.69 | convolution fusion | flops 2621603840 | bytes 14696448 | tf_op jit(solution)/shard_map/dot_general | solution.py:33
  124.4 8.6 %fusion.82 = bf16[256,640]{1,0:T(8,128)(2,1)S(1)} fusion(bf16[8000,640]{1,0:T(8,128)(2,1)} %all-gather.6.cloned.1.call-done, bf16[2,1000,8000]{2,1,0:T(8,128)(2,1)} %param.4), kind=kOutput, calls=%fused_computation.82 | convolution fusion | flops 2621603840 | bytes 14696448 | tf_op jit(solution)/shard_map/dot_general | solution.py:33
  133.0 8.6 %fusion.85 = bf16[256,640]{1,0:T(8,128)(2,1)S(1)} fusion(bf16[8000,640]{1,0:T(8,128)(2,1)} %all-gather.6.cloned.1.call-done, bf16[2,1000,8000]{2,1,0:T(8,128)(2,1)} %param.4), kind=kOutput, calls=%fused_computation.83 | convolution fusion | flops 2621603840 | bytes 14696448 | tf_op jit(solution)/shard_map/dot_general | solution.py:33
  143.1 8.7 %fusion.79 = bf16[256,640]{1,0:T(8,128)(2,1)S(1)} fusion(bf16[8000,640]{1,0:T(8,128)(2,1)} %all-gather.6.cloned.1.call-done, bf16[2,1000,8000]{2,1,0:T(8,128)(2,1)} %param.4), kind=kOutput, calls=%fused_computation.81 | convolution fusion | flops 2621603840 | bytes 14696448 | tf_op jit(solution)/shard_map/dot_general | solution.py:33
  151.9 9.6 %fusion.97 = (f32[]{:T(128)}, f32[]{:T(128)}, f32[]{:T(128)}, f32[]{:T(128)}, f32[]{:T(128)}, /*index=5*/f32[]{:T(128)}, bf16[256,640]{1,0:T(8,128)(2,1)S(1)}) fusion(bf16[256,640]{1,0:T(8,128)(2,1)S(1)} %fusion.48, bf16[1000,640]{1,0:T(8,128)(2,1)} %param.5, bf16[256,640]{1,0:T(8,128)(2,1)S(1)} %fusion.51, bf16[256,640]{1,0:T(8,128)(2,1)S(1)} %fusion.82, ...), kind=kOutput, calls=%fused_computation.170 | convolution fusion | flops 2625044480 | bytes 17317912 | tf_op jit(solution)/shard_map/dot_general | solution.py:33
  162.5 7.8 %copy.36 = f32[1000,2000]{1,0:T(8,128)} copy(f32[1000,2000]{1,0:T(8,128)} %param.6) | data formatting | bytes 16000000
  170.3 8.1 %fusion.88 = bf16[232,640]{1,0:T(8,128)(2,1)S(1)} fusion(bf16[8000,640]{1,0:T(8,128)(2,1)} %all-gather.6.cloned.1.call-done, bf16[2,1000,8000]{2,1,0:T(8,128)(2,1)} %param.4), kind=kOutput, calls=%fused_computation.84 | convolution fusion | flops 2375828480 | bytes 14278656 | tf_op jit(solution)/shard_map/dot_general | solution.py:33
  178.4 9.0 %fusion.103 = (f32[]{:T(128)}, f32[]{:T(128)}, bf16[232,640]{1,0:T(8,128)(2,1)S(1)}) fusion(bf16[1000,640]{1,0:T(8,128)(2,1)} %param.5, bf16[232,640]{1,0:T(8,128)(2,1)S(1)} %fusion.88, bf16[8000,640]{1,0:T(8,128)(2,1)} %all-gather.6.cloned.1.call-done, bf16[2,1000,8000]{2,1,0:T(8,128)(2,1)} %param.4), kind=kOutput, calls=%fused_computation.179 | convolution fusion | flops 2376867840 | bytes 14872584 | tf_op jit(solution)/shard_map/dot_general | solution.py:33
  187.4 5.2 fusion.124
  192.6 42.0 %psum.7 = f32[8]{0:T(128)S(1)} all-reduce(f32[8]{0:T(128)S(1)} %fusion.124), channel_id=1, replica_groups=mesh['grp'=4,'dev'=8] {'grp','dev'}, use_global_device_ids=true, to_apply=%region_8.0 | all-reduce | flops 8 | bytes 64 | tf_op jit(solution)/shard_map/psum | solution.py:47
  239.2 3.5 add_dynamic-update-slice_fusion.31
  242.7 4.1 add_dynamic-update-slice_fusion.30
  246.9 4.0 add_dynamic-update-slice_fusion.29
  250.8 4.0 add_dynamic-update-slice_fusion.28
  254.9 4.0 add_dynamic-update-slice_fusion.27
  258.9 4.1 add_dynamic-update-slice_fusion.26
  262.9 4.0 add_dynamic-update-slice_fusion.25
  267.0 4.0 add_dynamic-update-slice_fusion.24
  271.0 5.8 %dynamic-slice_bitcast_fusion.25 = (f32[1000,256]{1,0:T(8,128)S(1)}, f32[1000,256]{1,0:T(8,128)S(1)}, f32[1000,256]{1,0:T(8,128)}, f32[1000,256]{1,0:T(8,128)}, ...) fusion(f32[8,1000,256]{2,1,0:T(8,128)} %add_dynamic-update-slice_fusion.24, ...), kind=kLoop, calls=%fused_computation.123 | loop fusion | bytes 16384032 | tf_op jit(solution)/shard_map/squeeze | solution.py:73
  276.8 5.4 %fusion.24 = bf16[1000,512]{1,0:T(8,128)(2,1)} fusion(f32[1000,256]{1,0:T(8,128)} %get-tuple-element.123, f32[1000,256]{1,0:T(8,128)} %get-tuple-element.120, bf16[1000,1280]{1,0:T(8,128)(2,1)} %constant_dynamic-update-slice_fusion, bf16[2048,1280]{1,0:T(8,128)(2,1)} %all-gather.8.cloned.1.call-done, s32[]{:T(128)S(6)} %select_n.26), kind=kOutput, calls=%fused_computation.25 | convolution fusion | flops 1312256000 | bytes 6942724 | tf_op jit(solution)/shard_map/dot_general | solution.py:69
  282.3 4.3 fusion.25
  286.6 4.3 fusion.26
  290.9 3.3 maximum_subtract_fusion.3
  304.4 3.1 add_dynamic-update-slice_fusion.21
  307.4 3.1 add_dynamic-update-slice_fusion.20
  310.6 3.1 add_dynamic-update-slice_fusion.19
  313.7 3.1 add_dynamic-update-slice_fusion.18
  319.8 3.3 add_dynamic-update-slice_fusion.16
  326.1 5.4 fusion.27
  331.6 4.4 fusion.28
  336.0 4.3 fusion.29
  340.3 4.7 maximum_subtract_fusion.7
  351.7 3.1 add_dynamic-update-slice_fusion.14
  354.8 3.1 add_dynamic-update-slice_fusion.13
  357.9 3.1 add_dynamic-update-slice_fusion.12
  361.0 3.1 add_dynamic-update-slice_fusion.11
  367.2 3.1 add_dynamic-update-slice_fusion.9
  376.4 5.3 fusion.30
  381.8 4.4 fusion.31
  386.2 4.7 fusion.32
  390.9 4.7 maximum_subtract_fusion.11
  402.4 3.1 add_dynamic-update-slice_fusion.6
  405.5 3.1 add_dynamic-update-slice_fusion.5
  408.7 3.1 add_dynamic-update-slice_fusion.4
  411.8 3.1 add_dynamic-update-slice_fusion.3
  414.9 3.1 add_dynamic-update-slice_fusion.2
  418.1 3.1 add_dynamic-update-slice_fusion.1
  421.2 3.1 add_dynamic-update-slice_fusion
  427.3 5.3 fusion.33
  432.7 4.4 fusion.34
  437.1 4.4 fusion.35
  441.5 4.6 maximum_subtract_fusion.15
  458.2 3.3 slice_add_fusion.6
  461.5 6.7 %dynamic_update_slice.29 = f32[1000,2000]{1,0:T(8,128)} dynamic-update-slice(f32[1000,2000]{1,0:T(8,128)} %get-tuple-element.92, f32[1000,256]{1,0:T(8,128)S(1)} %get-tuple-element.91, s32[]{:T(128)} %constant.3.clone.1, s32[]{:T(128)} %constant.10.clone.1) | dynamic-update-slice | bytes 2048004 | tf_op jit(solution)/shard_map/dynamic_update_slice | solution.py:88
  473.7 3.2 slice_add_fusion.4
  476.9 6.5 %dynamic_update_slice.31 = f32[1000,2000]{1,0:T(8,128)} dynamic-update-slice(f32[1000,2000]{1,0:T(8,128)} %get-tuple-element.90, f32[1000,256]{1,0:T(8,128)S(1)} %get-tuple-element.89, s32[]{:T(128)} %constant.3.clone.1, s32[]{:T(128)} %constant.12.clone.1) | dynamic-update-slice | bytes 2048004 | tf_op jit(solution)/shard_map/dynamic_update_slice | solution.py:88
  485.0 3.9 collective-permute-done.10
  499.7 11.1 %collective-permute-done.6 = bf16[1000,512]{1,0:T(8,128)(2,1)} collective-permute-done((bf16[1000,512]{1,0:T(8,128)(2,1)}, bf16[1000,512]{1,0:T(8,128)(2,1)}, u32[]{:S(2)}, u32[]{:S(2)}) %collective-permute-start.6) | collective-permute-done | bytes 1024032 | tf_op jit(solution)/shard_map/ppermute | solution.py:78
  513.3 3.2 slice_add_fusion.2
  516.4 6.5 %dynamic_update_slice.33 = f32[1000,2000]{1,0:T(8,128)} dynamic-update-slice(f32[1000,2000]{1,0:T(8,128)} %get-tuple-element.88, f32[1000,256]{1,0:T(8,128)S(1)} %get-tuple-element.87, s32[]{:T(128)} %constant.3.clone.1, s32[]{:T(128)} %constant.13.clone.1) | dynamic-update-slice | bytes 2048004 | tf_op jit(solution)/shard_map/dynamic_update_slice | solution.py:88
  522.9 5.7 %dynamic_update_slice.34 = f32[1000,2000]{1,0:T(8,128)} dynamic-update-slice(f32[1000,2000]{1,0:T(8,128)} %dynamic_update_slice.33, f32[1000,232]{1,0:T(8,128)S(1)} %get-tuple-element.86, s32[]{:T(128)} %constant.3.clone.1, s32[]{:T(128)} %constant.16.clone.1) | dynamic-update-slice | bytes 1856004 | tf_op jit(solution)/shard_map/dynamic_update_slice | solution.py:88
  528.6 6.3 %dynamic_update_slice.35 = f32[1000,2000]{1,0:T(8,128)} dynamic-update-slice(f32[1000,2000]{1,0:T(8,128)} %dynamic_update_slice.34, f32[1000,232]{1,0:T(8,128)S(1)} %get-tuple-element.85, s32[]{:T(128)} %constant.3.clone.1, s32[]{:T(128)} %constant.17.clone.1) | dynamic-update-slice | bytes 1856004 | tf_op jit(solution)/shard_map/dynamic_update_slice | solution.py:88
  (136 shorter events, 83.1 us)
Async XLA Ops:
  6.5 228.2 %copy-start = (f32[8,8]{1,0:T(8,128)S(1)}, f32[8,8]{1,0:T(8,128)}, u32[]{:S(2)}) copy-start(f32[8,8]{1,0:T(8,128)} %param.7) | copy-start | bytes 772
  6.5 102.6 %all-gather.6.cloned.1.call-start = ((), (), s32[]{:S(2)}) async-start(), calls=%async_computation | async-start | bytes 11520000 | tf_op jit(solution)/shard_map/all_gather | solution.py:26
  7.3 269.6 %all-gather.8.cloned.1.call-start = ((), (), s32[]{:S(2)}) async-start(), calls=%async_computation.1 | async-start | bytes 5898240 | tf_op jit(solution)/shard_map/all_gather | solution.py:41
  109.1 8.7 %copy-start.27 = (bf16[8000,640]{1,0:T(8,128)(2,1)S(1)}, bf16[8000,640]{1,0:T(8,128)(2,1)}, u32[]{:S(2)}) copy-start(bf16[8000,640]{1,0:T(8,128)(2,1)} %all-gather.6.cloned.1.call-done) | copy-start | bytes 30720004
  124.3 201.8 %all-gather.10.cloned.1.call-start = ((), (), s32[]{:S(2)}) async-start(), calls=%async_computation.2 | async-start | bytes 5898240 | tf_op jit(solution)/shard_map/all_gather | solution.py:41
  142.6 233.8 %all-gather.12.cloned.1.call-start = ((), (), s32[]{:S(2)}) async-start(), calls=%async_computation.3 | async-start | bytes 5898240 | tf_op jit(solution)/shard_map/all_gather | solution.py:41
  162.4 264.9 %all-gather.14.cloned.1.call-start = ((), (), s32[]{:S(2)}) async-start(), calls=%async_computation.4 | async-start | bytes 5345280 | tf_op jit(solution)/shard_map/all_gather | solution.py:41
  178.4 57.2 %copy-start.4 = (bf16[256,1280]{1,0:T(8,128)(2,1)S(1)}, bf16[256,1280]{1,0:T(8,128)(2,1)}, u32[]{:S(2)}) copy-start(bf16[256,1280]{1,0:T(8,128)(2,1)} %pad_maximum_fusion) | copy-start | bytes 1966084
  178.4 58.1 %copy-start.3 = (bf16[256,1280]{1,0:T(8,128)(2,1)S(1)}, bf16[256,1280]{1,0:T(8,128)(2,1)}, u32[]{:S(2)}) copy-start(bf16[256,1280]{1,0:T(8,128)(2,1)} %pad_maximum_fusion.1) | copy-start | bytes 1966084
  187.4 50.0 %copy-start.2 = (bf16[256,1280]{1,0:T(8,128)(2,1)S(1)}, bf16[256,1280]{1,0:T(8,128)(2,1)}, u32[]{:S(2)}) copy-start(bf16[256,1280]{1,0:T(8,128)(2,1)} %pad_maximum_fusion.2) | copy-start | bytes 1966084
  234.7 12.1 %copy-start.5 = (bf16[232,1280]{1,0:T(8,128)(2,1)}, bf16[232,1280]{1,0:T(8,128)(2,1)S(1)}, u32[]{:S(2)}) copy-start(bf16[232,1280]{1,0:T(8,128)(2,1)S(1)} %pad_maximum_fusion.3) | copy-start | bytes 1781764
  276.8 5.4 %copy-start.22 = (f32[1000,256]{1,0:T(8,128)S(1)}, f32[1000,256]{1,0:T(8,128)}, u32[]{:S(2)}) copy-start(f32[1000,256]{1,0:T(8,128)} %get-tuple-element.119) | copy-start | bytes 3072004
  276.8 5.4 %copy-start.23 = (f32[1000,256]{1,0:T(8,128)S(1)}, f32[1000,256]{1,0:T(8,128)}, u32[]{:S(2)}) copy-start(f32[1000,256]{1,0:T(8,128)} %get-tuple-element.122) | copy-start | bytes 3072004
  276.8 5.4 %copy-start.30 = (bf16[2048,1280]{1,0:T(8,128)(2,1)S(1)}, bf16[2048,1280]{1,0:T(8,128)(2,1)}, u32[]{:S(2)}) copy-start(bf16[2048,1280]{1,0:T(8,128)(2,1)} %all-gather.8.cloned.1.call-done) | copy-start | bytes 15728644
  286.6 4.3 copy-start.16
  294.2 53.4 %collective-permute-start = (bf16[1000,512]{1,0:T(8,128)(2,1)}, bf16[1000,512]{1,0:T(8,128)(2,1)}, u32[]{:S(2)}, u32[]{:S(2)}) collective-permute-start(bf16[1000,512]{1,0:T(8,128)(2,1)} %fusion.24), channel_id=1, source_target_pairs={{0,8},{8,0},{16,24},{24,16},{1,9},{9,1},{17,25},{25,17},{2,10},{10... | collective-permute-start | bytes 3072008 | tf_op jit(solution)/shard_map/ppermute | solution.py:78
  296.4 52.1 %collective-permute-start.1 = (bf16[1000,512]{1,0:T(8,128)(2,1)}, bf16[1000,512]{1,0:T(8,128)(2,1)}, u32[]{:S(2)}, u32[]{:S(2)}) collective-permute-start(bf16[1000,512]{1,0:T(8,128)(2,1)} %fusion.25), channel_id=1, source_target_pairs={{0,16},{8,24},{16,0},{24,8},{1,17},{9,25},{17,1},{25,9},{2,18},{10... | collective-permute-start | bytes 3072008 | tf_op jit(solution)/shard_map/ppermute | solution.py:78
  297.2 51.3 %collective-permute-start.2 = (bf16[1000,512]{1,0:T(8,128)(2,1)}, bf16[1000,512]{1,0:T(8,128)(2,1)}, u32[]{:S(2)}, u32[]{:S(2)}) collective-permute-start(bf16[1000,512]{1,0:T(8,128)(2,1)} %fusion.26), channel_id=1, source_target_pairs={{0,24},{8,16},{16,8},{24,0},{1,25},{9,17},{17,9},{25,1},{2,26},{10... | collective-permute-start | bytes 3072008 | tf_op jit(solution)/shard_map/ppermute | solution.py:78
  326.1 5.4 copy-start.24
  326.1 5.4 copy-start.25
  326.1 5.4 copy-start.29
  331.5 4.5 copy-start.20
  331.5 4.5 copy-start.21
  336.0 4.3 copy-start.17
  345.0 54.0 %collective-permute-start.3 = (bf16[1000,512]{1,0:T(8,128)(2,1)}, bf16[1000,512]{1,0:T(8,128)(2,1)}, u32[]{:S(2)}, u32[]{:S(2)}) collective-permute-start(bf16[1000,512]{1,0:T(8,128)(2,1)} %fusion.27), channel_id=1, source_target_pairs={{0,8},{8,0},{16,24},{24,16},{1,9},{9,1},{17,25},{25,17},{2,10},{10... | collective-permute-start | bytes 3072008 | tf_op jit(solution)/shard_map/ppermute | solution.py:78
  347.0 52.0 %collective-permute-start.4 = (bf16[1000,512]{1,0:T(8,128)(2,1)}, bf16[1000,512]{1,0:T(8,128)(2,1)}, u32[]{:S(2)}, u32[]{:S(2)}) collective-permute-start(bf16[1000,512]{1,0:T(8,128)(2,1)} %fusion.28), channel_id=1, source_target_pairs={{0,16},{8,24},{16,0},{24,8},{1,17},{9,25},{17,1},{25,9},{2,18},{10... | collective-permute-start | bytes 3072008 | tf_op jit(solution)/shard_map/ppermute | solution.py:78
  347.6 51.4 %collective-permute-start.5 = (bf16[1000,512]{1,0:T(8,128)(2,1)}, bf16[1000,512]{1,0:T(8,128)(2,1)}, u32[]{:S(2)}, u32[]{:S(2)}) collective-permute-start(bf16[1000,512]{1,0:T(8,128)(2,1)} %fusion.29), channel_id=1, source_target_pairs={{0,24},{8,16},{16,8},{24,0},{1,25},{9,17},{17,9},{25,1},{2,26},{10... | collective-permute-start | bytes 3072008 | tf_op jit(solution)/shard_map/ppermute | solution.py:78
  376.4 5.3 copy-start.18
  376.4 5.3 copy-start.19
  376.4 5.3 copy-start.28
  381.7 4.4 copy-start.14
  381.7 4.4 copy-start.15
  386.2 4.7 copy-start.13
  395.5 104.2 %collective-permute-start.8 = (bf16[1000,512]{1,0:T(8,128)(2,1)}, bf16[1000,512]{1,0:T(8,128)(2,1)}, u32[]{:S(2)}, u32[]{:S(2)}) collective-permute-start(bf16[1000,512]{1,0:T(8,128)(2,1)} %fusion.32), channel_id=1, source_target_pairs={{0,24},{8,16},{16,8},{24,0},{1,25},{9,17},{17,9},{25,1},{2,26},{10... | collective-permute-start | bytes 3072008 | tf_op jit(solution)/shard_map/ppermute | solution.py:78
  397.6 102.2 %collective-permute-start.7 = (bf16[1000,512]{1,0:T(8,128)(2,1)}, bf16[1000,512]{1,0:T(8,128)(2,1)}, u32[]{:S(2)}, u32[]{:S(2)}) collective-permute-start(bf16[1000,512]{1,0:T(8,128)(2,1)} %fusion.31), channel_id=1, source_target_pairs={{0,16},{8,24},{16,0},{24,8},{1,17},{9,25},{17,1},{25,9},{2,18},{10... | collective-permute-start | bytes 3072008 | tf_op jit(solution)/shard_map/ppermute | solution.py:78
  427.3 5.4 copy-start.11
  427.3 5.4 copy-start.12
  427.3 5.4 copy-start.31
  432.7 4.4 copy-start.9
  432.7 4.4 copy-start.10
  437.1 4.4 copy-start.8
  446.1 6.1 %copy-start.26 = (bf16[1000,464]{1,0:T(8,128)(2,1)S(1)}, bf16[1000,464]{1,0:T(8,128)(2,1)}, u32[]{:S(2)}) copy-start(bf16[1000,464]{1,0:T(8,128)(2,1)} %fusion.33) | copy-start | bytes 2784004
  448.4 25.2 %collective-permute-start.11 = (bf16[1000,464]{0,1:T(8,128)(2,1)}, bf16[1000,464]{0,1:T(8,128)(2,1)}, u32[]{:S(2)}, u32[]{:S(2)}) collective-permute-start(bf16[1000,464]{0,1:T(8,128)(2,1)} %copy.9), channel_id=1, source_target_pairs={{0,24},{8,16},{16,8},{24,0},{1,25},{9,17},{17,9},{25,1},{2,26},{10... | collective-permute-start | bytes 2784008 | tf_op jit(solution)/shard_map/ppermute | solution.py:78
  452.2 36.8 %collective-permute-start.10 = (bf16[1000,464]{0,1:T(8,128)(2,1)}, bf16[1000,464]{0,1:T(8,128)(2,1)}, u32[]{:S(2)}, u32[]{:S(2)}) collective-permute-start(bf16[1000,464]{0,1:T(8,128)(2,1)} %copy.7), channel_id=1, source_target_pairs={{0,16},{8,24},{16,0},{24,8},{1,17},{9,25},{17,1},{25,9},{2,18},{10... | collective-permute-start | bytes 2784008 | tf_op jit(solution)/shard_map/ppermute | solution.py:78
  453.7 39.4 %collective-permute-start.9 = (bf16[1000,464]{0,1:T(8,128)(2,1)}, bf16[1000,464]{0,1:T(8,128)(2,1)}, u32[]{:S(2)}, u32[]{:S(2)}) collective-permute-start(bf16[1000,464]{0,1:T(8,128)(2,1)} %copy.5), channel_id=1, source_target_pairs={{0,8},{8,0},{16,24},{24,16},{1,9},{9,1},{17,25},{25,17},{2,10},{10... | collective-permute-start | bytes 2784008 | tf_op jit(solution)/shard_map/ppermute | solution.py:78
  458.2 10.0 %copy-start.6 = (f32[1000,512]{1,0:T(8,128)S(1)}, f32[1000,512]{1,0:T(8,128)}, u32[]{:S(2)}) copy-start(f32[1000,512]{1,0:T(8,128)} %maximum_subtract_fusion.7) | copy-start | bytes 6144004
  473.6 37.2 %collective-permute-start.6 = (bf16[1000,512]{1,0:T(8,128)(2,1)}, bf16[1000,512]{1,0:T(8,128)(2,1)}, u32[]{:S(2)}, u32[]{:S(2)}) collective-permute-start(bf16[1000,512]{1,0:T(8,128)(2,1)} %fusion.30), channel_id=1, source_target_pairs={{0,8},{8,0},{16,24},{24,16},{1,9},{9,1},{17,25},{25,17},{2,10},{10... | collective-permute-start | bytes 3072008 | tf_op jit(solution)/shard_map/ppermute | solution.py:78
  497.1 13.8 %copy-start.7 = (f32[1000,512]{1,0:T(8,128)S(1)}, f32[1000,512]{1,0:T(8,128)}, u32[]{:S(2)}) copy-start(f32[1000,512]{1,0:T(8,128)} %maximum_subtract_fusion.11) | copy-start | bytes 6144004
  513.2 21.7 %copy-start.1 = (f32[8,8]{1,0:T(8,128)S(1)}, f32[8,8]{1,0:T(8,128)}, u32[]{:S(2)}) copy-start(f32[8,8]{1,0:T(8,128)} %param.7) | copy-start | bytes 772
Sparse Core Ops, SparseCore 0:
  9.0 100.0 all-gather.5
  124.5 54.4 all-gather.7
  180.6 55.8 all-gather.9
  237.9 54.8 all-gather.11
  294.4 50.7 all-gather.13
